TPU v7x, 32 devices: a whole 2x2x4 slice. The times are simulated.
32 devices in a mesh: groups: 2 (over y), dp: 4 (over x, core), tensor: 4 (over z).
Axes of the slice: x: 2, y: 2, z: 4, core: 2. Of those that a mesh axis runs over, the one named last changes fastest.
Arguments:
- tokens: bfloat16 [4096, 8192], P(('groups', 'dp'), 'tensor'), parts along dimension 0, may hold values from -6 to 6
- cotangent: bfloat16 [4096, 8192], P(('groups', 'dp'), 'tensor'), parts along dimension 0, may hold values from -6 to 6
- segment: int32 [4096], P(('groups', 'dp')), parts along dimension 0, may hold values from 0 to 15, never falling along the last dimension, each value on 1 to 512 neighbouring positions
- owner_slot: int32 [32], P('groups'), parts along dimension 0, may hold values from 0 to 15, each once
- out_weight: bfloat16 [8192, 8192], P(None, 'tensor'), may hold values from -0.0625 to 0.0625
- a_weight: float32 [32, 8192, 64], P(('groups', 'dp'), 'tensor'), parts along dimension 0, may hold values from -0.0625 to 0.0625
- b_weight: float32 [32, 64, 8192], P(('groups', 'dp'), None, 'tensor'), parts along dimension 0, may hold values from -0.75 to 0.75
- a_first: float32 [32, 8192, 64], P(('groups', 'dp'), 'tensor'), parts along dimension 0, may hold values from -1.5 to 1.5
- a_second: float32 [32, 8192, 64], P(('groups', 'dp'), 'tensor'), parts along dimension 0, may hold values from 0.001 to 0.1
- b_first: float32 [32, 64, 8192], P(('groups', 'dp'), None, 'tensor'), parts along dimension 0, may hold values from -0.15 to 0.15
- b_second: float32 [32, 64, 8192], P(('groups', 'dp'), None, 'tensor'), parts along dimension 0, may hold values from 1e-06 to 0.0001
Outputs:
- output: bfloat16 [4096, 8192], P(('groups', 'dp'), 'tensor'), parts along dimension 0
- token_input_gradient: bfloat16 [4096, 8192], P(('groups', 'dp'), 'tensor'), parts along dimension 0
- new_a: float32 [32, 8192, 64], P(('groups', 'dp'), 'tensor'), parts along dimension 0
- new_b: float32 [32, 64, 8192], P(('groups', 'dp'), None, 'tensor'), parts along dimension 0
- new_a_first: float32 [32, 8192, 64], P(('groups', 'dp'), 'tensor'), parts along dimension 0
- new_a_second: float32 [32, 8192, 64], P(('groups', 'dp'), 'tensor'), parts along dimension 0
- new_b_first: float32 [32, 64, 8192], P(('groups', 'dp'), None, 'tensor'), parts along dimension 0
- new_b_second: float32 [32, 64, 8192], P(('groups', 'dp'), None, 'tensor'), parts along dimension 0
There are 2 independent parts, one for each index of `groups`. A program takes and returns all parts, laid end to end along the dimension named above; an argument that names none is the same for every part. Nothing has to cross between parts.
Inputs may be any that keep to these rules, and one draw needn't show every extreme that they name: `segment`: job numbers never fall along the packed tokens; every job has at least one token and some job exactly 512. `owner_slot`: each slot holds exactly one job.
All inputs are finite; a program needn't handle non-finite values.
Results may differ from a plain program's by a relative error of at most 0.0045.
Values may be sent and summed in bfloat16 or wider, within the bound.
A program may use at most 256 MiB of HBM per device.

v0:
```python
import jax
import jax.numpy as jnp
from jax import lax
from jax.sharding import PartitionSpec as P

adapter_scale = 0.5
learn_rate = 0.01
beta_first = 0.9
beta_second = 0.999
adam_eps = 1e-08


def adam_step(weight, first, second, grad):
    first_new = beta_first * first + (1.0 - beta_first) * grad
    second_new = beta_second * second + (1.0 - beta_second) * grad * grad
    corr_first = 1.0 - beta_first**10
    corr_second = 1.0 - beta_second**10
    weight_new = weight - learn_rate * (first_new / corr_first) / (
        jnp.sqrt(second_new / corr_second) + adam_eps
    )
    return (weight_new, first_new, second_new)


def select_rows(wide, onehot, jobs_all, rank):
    return jnp.einsum("tjk,tj->tk", wide.reshape(wide.shape[0], jobs_all, rank), onehot)


def spread_rows(values, onehot):
    rows = values.shape[0]
    wide = onehot[:, :, None] * values.astype(jnp.float32)[:, None, :]
    return wide.reshape(rows, -1).astype(jnp.bfloat16)


def per_device(
    tokens,
    cotangent,
    segment,
    owner_slot,
    out_weight,
    a_weight,
    b_weight,
    a_first,
    a_second,
    b_first,
    b_second,
):
    local_width = tokens.shape[1]
    rank = a_weight.shape[2]
    jobs_all = owner_slot.shape[0]
    job_slot = owner_slot[segment]
    onehot = (job_slot[:, None] == jnp.arange(jobs_all, dtype=jnp.int32)[None, :]).astype(
        jnp.float32
    )
    a_half = a_weight.astype(jnp.bfloat16)
    adapter_b_half = b_weight.astype(jnp.bfloat16)
    a_every, b_every = (
        lax.all_gather(a_half, "dp", axis=0, tiled=True),
        lax.all_gather(adapter_b_half, "dp", axis=0, tiled=True),
    )
    adapter_a_flat = jnp.transpose(a_every, (1, 0, 2)).reshape(local_width, jobs_all * rank)
    adapter_b_flat = b_every.reshape(jobs_all * rank, local_width)
    down_part = select_rows(
        jnp.dot(tokens, adapter_a_flat, preferred_element_type=jnp.float32), onehot, jobs_all, rank
    )
    up_part = select_rows(
        lax.dot_general(
            cotangent, adapter_b_flat, (((1,), (1,)), ((), ())), preferred_element_type=jnp.float32
        ),
        onehot,
        jobs_all,
        rank,
    )
    down_proj = lax.psum(down_part, "tensor")
    down_product_wide = spread_rows(down_proj.astype(jnp.bfloat16), onehot)
    weight_rows = out_weight
    frozen_output = jnp.dot(
        lax.all_gather(tokens, "tensor", axis=1, tiled=True),
        weight_rows,
        preferred_element_type=jnp.float32,
    )
    adapter_output = jnp.dot(down_product_wide, adapter_b_flat, preferred_element_type=jnp.float32)
    output = (frozen_output + adapter_scale * adapter_output).astype(jnp.bfloat16)
    up_proj = lax.psum(up_part, "tensor")
    up_product_wide = spread_rows(up_proj.astype(jnp.bfloat16), onehot)
    weight_rows = out_weight
    frozen_backward = jnp.transpose(
        lax.psum_scatter(
            lax.dot_general(
                weight_rows, cotangent, (((1,), (1,)), ((), ())), preferred_element_type=jnp.float32
            ),
            "tensor",
            scatter_dimension=0,
            tiled=True,
        )
    )
    adapter_backward = lax.dot_general(
        up_product_wide,
        adapter_a_flat,
        (((1,), (1,)), ((), ())),
        preferred_element_type=jnp.float32,
    )
    token_input_gradient = (frozen_backward + adapter_scale * adapter_backward).astype(jnp.bfloat16)
    grad_a_part = lax.dot_general(
        tokens, up_product_wide, (((0,), (0,)), ((), ())), preferred_element_type=jnp.float32
    )
    grad_a_part = jnp.transpose(grad_a_part.reshape(local_width, jobs_all, rank), (1, 0, 2))
    grad_b_part = lax.dot_general(
        down_product_wide, cotangent, (((0,), (0,)), ((), ())), preferred_element_type=jnp.float32
    )
    grad_b_part = grad_b_part.reshape(jobs_all, rank, local_width)
    count_part = jnp.sum(onehot, axis=0)
    grad_a, grad_b, token_counts = (
        lax.psum_scatter(grad_a_part, "dp", scatter_dimension=0, tiled=True),
        lax.psum_scatter(grad_b_part, "dp", scatter_dimension=0, tiled=True),
        lax.psum_scatter(count_part, "dp", scatter_dimension=0, tiled=True),
    )
    scale_factor = adapter_scale / token_counts
    grad_a = grad_a * scale_factor[:, None, None]
    grad_b = grad_b * scale_factor[:, None, None]
    new_a, new_a_first, new_a_second = adam_step(a_weight, a_first, a_second, grad_a)
    new_b, new_b_first, new_b_second = adam_step(b_weight, b_first, b_second, grad_b)
    return (
        output,
        token_input_gradient,
        new_a,
        new_b,
        new_a_first,
        new_a_second,
        new_b_first,
        new_b_second,
    )


def solution(mesh):
    return jax.shard_map(
        per_device,
        mesh=mesh,
        in_specs=(
            P(("groups", "dp"), "tensor"),
            P(("groups", "dp"), "tensor"),
            P(("groups", "dp")),
            P("groups"),
            P(None, "tensor"),
            P(("groups", "dp"), "tensor", None),
            P(("groups", "dp"), None, "tensor"),
            P(("groups", "dp"), "tensor", None),
            P(("groups", "dp"), "tensor", None),
            P(("groups", "dp"), None, "tensor"),
            P(("groups", "dp"), None, "tensor"),
        ),
        out_specs=(
            P(("groups", "dp"), "tensor"),
            P(("groups", "dp"), "tensor"),
            P(("groups", "dp"), "tensor", None),
            P(("groups", "dp"), None, "tensor"),
            P(("groups", "dp"), "tensor", None),
            P(("groups", "dp"), "tensor", None),
            P(("groups", "dp"), None, "tensor"),
            P(("groups", "dp"), None, "tensor"),
        ),
        check_vma=False,
    )
```

profile of v0, /device:TPU:0, one launch (start us, length us, event | category | flops | bytes accessed | tf_op | source)
XLA Modules:
  0.0 684.5 jit_solution(1978188087229578397)
XLA Ops:
  7.2 2.9 convert_element_type.46
  10.2 2.7 convert_element_type.50
  13.0 0.7 all-gather.4.cloned.1.call-update
  13.7 0.7 fusion.33
  14.4 10.1 %select_select_fusion = s32[512]{0:T(512)S(1)} fusion(s32[512]{0:T(512)S(1)} %copy-done.5, s32[]{:T(128)} %bitcast, s32[]{:T(128)} %bitcast.1, s32[]{:T(128)} %bitcast.2, s32[]{:T(128)} %bitcast.3, s32[]{:T(128)} %bitcast.4, s32[]{:T(128)} %bitcast.5, s32[]{:T(128)} %bitcast.6, s32[]{:T(128)} %bitcast.7, s32[]{:T(128)} %bitcast.8, s32[]{:T(128)} %bitcast.9, ...), kind=kLoop, calls=%fused_computation.38 | loop fusion | flops 16896 | bytes 4160 | tf_op jit(solution)/shard_map/gather | solution.py:50
  24.5 22.9 %all-gather.6.cloned.1.call-done = bf16[16,2048,64]{1,2,0:T(8,128)(2,1)} async-done(((bf16[4,2048,64]{1,2,0:T(8,128)(2,1)}), bf16[16,2048,64]{1,2,0:T(8,128)(2,1)}) %all-gather.6.cloned.1.call-update) | async-done | bytes 4194320 | tf_op jit(solution)/shard_map/all_gather | solution.py:57
  47.4 5.2 multiply_reduce_fusion.1
  52.6 31.4 %all-gather.8.cloned.1.call-done = bf16[16,64,2048]{2,1,0:T(8,128)(2,1)} async-done(((bf16[4,64,2048]{2,1,0:T(8,128)(2,1)}), bf16[16,64,2048]{2,1,0:T(8,128)(2,1)}) %all-gather.8.cloned.1.call-update) | async-done | bytes 4194320 | tf_op jit(solution)/shard_map/all_gather | solution.py:58
  84.1 4.6 multiply_reduce_fusion
  88.7 33.1 %all-reduce.3 = (bf16[512,64]{0,1:T(8,128)(2,1)S(1)}, bf16[512,64]{0,1:T(8,128)(2,1)S(1)}) all-reduce(f32[512,64]{0,1:T(8,128)S(1)} %multiply_reduce_fusion.1, f32[512,64]{0,1:T(8,128)S(1)} %multiply_reduce_fusion), channel_id=1, replica_groups=mesh['groups'=2,'dp'=4,'tensor'=4] {'tensor'}, use_global_device_ids=true, to_apply=%region_0.0 | all-reduce | flops 65536 | bytes 393216 | tf_op jit(solution)/shard_map/psum | solution.py:73
  122.0 7.2 %fusion.36 = f32[1024,2048]{1,0:T(8,128)} fusion(bf16[512,1024]{0,1:T(8,128)(2,1)S(1)} %bitcast.80, bf16[512,2048]{1,0:T(8,128)(2,1)} %param.11), kind=kOutput, calls=%fused_computation.43 | convolution fusion | flops 2147483648 | bytes 11534336 | tf_op jit(solution)/shard_map/dot_general | solution.py:103
  129.3 5.5 fusion.12
  135.1 26.7 %fusion.35 = f32[8192,512]{0,1:T(8,128)} fusion(bf16[8192,2048]{1,0:T(8,128)(2,1)} %param.15, bf16[512,2048]{1,0:T(8,128)(2,1)S(1)} %copy-done), kind=kOutput, calls=%fused_computation.42 | convolution fusion | flops 17179869184 | bytes 52428800 | tf_op jit(solution)/shard_map/dot_general | solution.py:88
  161.8 0.6 copy-done.6
  163.8 6.3 all-reduce
  170.2 70.7 %all-gather.4.cloned.1.call-done = bf16[512,8192]{1,0:T(8,128)(2,1)} async-done(((bf16[512,2048]{1,0:T(8,128)(2,1)}), bf16[512,8192]{1,0:T(8,128)(2,1)}) %all-gather.4.cloned.1.call-update) | async-done | bytes 8388624 | tf_op jit(solution)/shard_map/all_gather | solution.py:77
  240.9 24.7 %fusion.34 = f32[512,2048]{1,0:T(8,128)S(1)} fusion(bf16[512,8192]{1,0:T(8,128)(2,1)} %all-gather.4.cloned.1.call-done, bf16[8192,2048]{1,0:T(8,128)(2,1)} %param.15), kind=kOutput, calls=%fused_computation.41 | convolution fusion | flops 17179869184 | bytes 46137344 | tf_op jit(solution)/shard_map/dot_general | solution.py:76
  265.6 3.7 fusion.5
  269.4 44.1 %reduce-scatter.6.cloned.1.call-done = f32[4,2048,64]{1,2,0:T(8,128)} async-done(((f32[16,2048,64]{1,2,0:T(8,128)}), f32[4,2048,64]{1,2,0:T(8,128)}) %reduce-scatter.6.cloned.1.call-update) | async-done | bytes 2097168 | tf_op jit(solution)/shard_map/reduce_scatter | solution.py:113
  313.4 6.7 divide_subtract_fusion.1
  320.2 67.7 %reduce-scatter.8.cloned.1.call-done = f32[4,64,2048]{2,1,0:T(8,128)} async-done(((f32[16,64,2048]{2,1,0:T(8,128)}), f32[4,64,2048]{2,1,0:T(8,128)}) %reduce-scatter.8.cloned.1.call-update) | async-done | bytes 2097168 | tf_op jit(solution)/shard_map/reduce_scatter | solution.py:114
  387.8 7.3 %divide_subtract_fusion = (f32[4,64,2048]{2,1,0:T(8,128)}, f32[4,64,2048]{2,1,0:T(8,128)}, f32[4,64,2048]{2,1,0:T(8,128)}) fusion(f32[4,64,2048]{2,1,0:T(8,128)} %param.17, f32[4,64,2048]{2,1,0:T(8,128)} %reduce-scatter.8.cloned.1.call-done, f32[4]{0:T(128)S(1)} %dynamic-slice_divide_fusion, f32[4,64,2048]{2,1,0:T(8,128)} %param.20, f32[4,64,2048]{2,1,0:T(8,128)} %param.21), kind=kLoop, calls=%fused_computation.21 | loop fusion | flops 6815744 | bytes 14680080 | tf_op jit(solution)/shard_map/sub | solution.py:18
  395.1 275.2 %reduce-scatter.4.cloned.1.call-done = f32[2048,512]{0,1:T(8,128)} async-done(((f32[8192,512]{0,1:T(8,128)}), f32[2048,512]{0,1:T(8,128)}) %reduce-scatter.4.cloned.1.call-update) | async-done | bytes 4194320 | tf_op jit(solution)/shard_map/reduce_scatter | solution.py:87
  670.4 7.3 %fusion.3 = bf16[512,2048]{1,0:T(8,128)(2,1)} fusion(f32[2048,512]{0,1:T(8,128)} %reduce-scatter.4.cloned.1.call-done, bf16[16,2048,64]{1,2,0:T(8,128)(2,1)} %all-gather.6.cloned.1.call-done, f32[512,64]{0,1:T(8,128)S(1)} %convert_element_type.74, f32[512,16]{0,1:T(8,128)S(1)} %fusion.29), kind=kOutput, calls=%fused_computation.4 | convolution fusion | flops 2151677952 | bytes 10649600 | tf_op jit(solution)/shard_map/dot_general | solution.py:96
  (31 shorter events, 1.6 us)
Async XLA Ops:
  7.2 76.9 %copy-start = (bf16[512,2048]{1,0:T(8,128)(2,1)S(1)}, bf16[512,2048]{1,0:T(8,128)(2,1)}, u32[]{:S(2)}) copy-start(bf16[512,2048]{1,0:T(8,128)(2,1)} %param.12) | copy-start | bytes 6291460
  7.2 40.3 %all-gather.6.cloned.1.call-start = ((), (), s32[]{:S(2)}) async-start(), calls=%async_computation.4 | async-start | bytes 5242880 | tf_op jit(solution)/shard_map/all_gather | solution.py:57
  10.1 74.0 %all-gather.8.cloned.1.call-start = ((), (), s32[]{:S(2)}) async-start(), calls=%async_computation.5 | async-start | bytes 5242880 | tf_op jit(solution)/shard_map/all_gather | solution.py:58
  12.9 0.8 copy-start.4
  12.9 1.5 copy-start.5
  12.9 228.0 %all-gather.4.cloned.1.call-start = ((), (), s32[]{:S(2)}) async-start(), calls=%async_computation.3 | async-start | bytes 10485760 | tf_op jit(solution)/shard_map/all_gather | solution.py:77
  13.6 299.8 %reduce-scatter.6.cloned.1.call-start = ((), (), s32[]{:S(2)}) async-start(), calls=%async_computation.7 | async-start | bytes 10485760 | tf_op jit(solution)/shard_map/reduce_scatter | solution.py:113
  129.2 258.6 %reduce-scatter.8.cloned.1.call-start = ((), (), s32[]{:S(2)}) async-start(), calls=%async_computation.8 | async-start | bytes 10485760 | tf_op jit(solution)/shard_map/reduce_scatter | solution.py:114
  134.8 535.5 %reduce-scatter.4.cloned.1.call-start = ((), (), s32[]{:S(2)}) async-start(), calls=%async_computation.6 | async-start | bytes 20971520 | tf_op jit(solution)/shard_map/reduce_scatter | solution.py:87
  161.8 0.7 copy-start.6
  240.9 24.7 %copy-start.3 = (bf16[16,64,2048]{2,1,0:T(8,128)(2,1)S(1)}, bf16[16,64,2048]{2,1,0:T(8,128)(2,1)}, u32[]{:S(2)}) copy-start(bf16[16,64,2048]{2,1,0:T(8,128)(2,1)} %all-gather.8.cloned.1.call-done) | copy-start | bytes 12582916
  265.6 47.8 %copy-start.2 = (f32[4,2048,64]{1,2,0:T(8,128)S(1)}, f32[4,2048,64]{1,2,0:T(8,128)}, u32[]{:S(2)}) copy-start(f32[4,2048,64]{1,2,0:T(8,128)} %param.16) | copy-start | bytes 6291460
  670.4 7.3 %copy-start.1 = (bf16[512,2048]{1,0:T(8,128)(2,1)S(1)}, bf16[512,2048]{1,0:T(8,128)(2,1)}, u32[]{:S(2)}) copy-start(bf16[512,2048]{1,0:T(8,128)(2,1)} %param.12) | copy-start | bytes 6291460
Sparse Core Ops, SparseCore 0:
  10.2 37.1 all-gather.5
  49.6 34.4 all-gather.7
  85.7 155.1 all-gather.3
  243.3 70.0 reduce-scatter.5
  316.0 71.7 reduce-scatter.7
  390.0 280.2 reduce-scatter.3
where the time goes:
time: 685 us
  waiting for transfers between devices  513 us (75%)
  matrix products  85 us (12%)
  blocking collectives  39.4 us (6%)
  other arithmetic  30.1 us (4%)
  between operations  14.9 us (2%)
    reduce_scatter x1, waiting for transfers between devices, per_device(): lax.psum_scatter(lax.dot_general(weight_rows, cotangent, (((1,), (1,)), (...  275 us
    all_gather x1, waiting for transfers between devices, per_device(): lax.all_gather(tokens, 'tensor', axis=1, tiled=True)  70.7 us
    reduce_scatter x1, waiting for transfers between devices, per_device(): lax.psum_scatter(grad_b_part, 'dp', scatter_dimension=0, tiled=True)  67.7 us
    reduce_scatter x1, waiting for transfers between devices, per_device(): lax.psum_scatter(grad_a_part, 'dp', scatter_dimension=0, tiled=True)  44.1 us
    psum x1, blocking collectives, per_device(): down_proj = lax.psum(down_part, 'tensor')  33.1 us
    all_gather x1, waiting for transfers between devices, per_device(): lax.all_gather(adapter_b_half, 'dp', axis=0, tiled=True)  31.4 us
    dot_general x1, matrix products, per_device(): lax.dot_general(weight_rows, cotangent, (((1,), (1,)), ((), ())), preferr...  26.7 us
    dot_general x1, matrix products, per_device(): jnp.dot(lax.all_gather(tokens, 'tensor', axis=1, tiled=True), weight_rows...  24.7 us
  transfers between devices with their start and end apart: 6, of which 6 were waited for; matrix products, arithmetic and copies ran while one was open for 16% of the time, Pallas kernels for 0%

commit v1 on v0

--- a/solution.py
+++ b/solution.py
@@ -29,6 +29,82 @@
     rows = values.shape[0]
     wide = onehot[:, :, None] * values.astype(jnp.float32)[:, None, :]
     return wide.reshape(rows, -1).astype(jnp.bfloat16)
+
+
+def grouped_sums(tokens, cotangent, out_weight, size):
+    me = lax.axis_index("tensor")
+    rows, width = tokens.shape
+    partial = [
+        lax.dot_general(
+            cotangent,
+            out_weight[at * width : (at + 1) * width],
+            (((1,), (1,)), ((), ())),
+            preferred_element_type=jnp.float32,
+        ).astype(jnp.bfloat16)
+        for at in range(size)
+    ]
+    partial = jnp.stack(partial)
+    to_right = [(i, i + 1) for i in range(size - 1)]
+    to_left = [(i + 1, i) for i in range(size - 1)]
+    from_left, from_right = [], []
+
+    def outgoing(came, turn, place, towards):
+        owner = jnp.clip(me + towards * (size - turn), 0, size - 1)
+        own = lax.dynamic_index_in_dim(partial, owner, 0, keepdims=False)
+        own = jnp.where(turn > place, own.astype(jnp.float32), 0.0)
+        return (came.astype(jnp.float32) + own).astype(jnp.bfloat16)
+
+    for turn in range(size):
+        if turn == 0:
+            right, left = tokens, tokens
+        else:
+            right = outgoing(from_left[-1], turn, me, 1)
+            left = outgoing(from_right[-1], turn, size - 1 - me, -1)
+        from_left.append(lax.ppermute(right, "tensor", to_right))
+        from_right.append(lax.ppermute(left, "tensor", to_left))
+
+    def rows_of(block):
+        return lax.dynamic_slice_in_dim(out_weight, block * width, width, 0)
+
+    frozen = jnp.dot(tokens, rows_of(me), preferred_element_type=jnp.float32)
+    lower = me < size // 2
+    nearest = jnp.minimum(me, size - 1 - me)
+    step = jnp.where(lower, 1, -1)
+    for turn in range(size - 1):
+        block = jnp.where(lower, from_right[turn], from_left[turn])
+        owner = me + step * (turn + 1)
+        other = size - 2 - turn
+        if turn >= size // 2:
+            short = jnp.where(lower, from_left[other], from_right[other])
+            use_short = other < nearest
+            block = jnp.where(use_short, short, block)
+            owner = jnp.where(use_short, me - step * (other + 1), owner)
+        frozen = frozen + jnp.dot(block, rows_of(owner), preferred_element_type=jnp.float32)
+    own = lax.dynamic_index_in_dim(partial, me, 0, keepdims=False).astype(jnp.float32)
+    backward = (
+        own + from_left[-1].astype(jnp.float32) + from_right[-1].astype(jnp.float32)
+    )
+    return frozen, backward
+
+
+def base_products(tokens, cotangent, out_weight):
+    size = lax.axis_size("tensor")
+    if size % 2 == 0 and size <= 8:
+        return grouped_sums(tokens, cotangent, out_weight, size)
+    frozen_output = jnp.dot(
+        lax.all_gather(tokens, "tensor", axis=1, tiled=True),
+        out_weight,
+        preferred_element_type=jnp.float32,
+    )
+    frozen_backward = lax.psum_scatter(
+        lax.dot_general(
+            out_weight, cotangent, (((1,), (1,)), ((), ())), preferred_element_type=jnp.float32
+        ),
+        "tensor",
+        scatter_dimension=0,
+        tiled=True,
+    )
+    return frozen_output, jnp.transpose(frozen_backward)
 
 
 def per_device(
@@ -72,27 +148,11 @@
     )
     down_proj = lax.psum(down_part, "tensor")
     down_product_wide = spread_rows(down_proj.astype(jnp.bfloat16), onehot)
-    weight_rows = out_weight
-    frozen_output = jnp.dot(
-        lax.all_gather(tokens, "tensor", axis=1, tiled=True),
-        weight_rows,
-        preferred_element_type=jnp.float32,
-    )
+    frozen_output, frozen_backward = base_products(tokens, cotangent, out_weight)
     adapter_output = jnp.dot(down_product_wide, adapter_b_flat, preferred_element_type=jnp.float32)
     output = (frozen_output + adapter_scale * adapter_output).astype(jnp.bfloat16)
     up_proj = lax.psum(up_part, "tensor")
     up_product_wide = spread_rows(up_proj.astype(jnp.bfloat16), onehot)
-    weight_rows = out_weight
-    frozen_backward = jnp.transpose(
-        lax.psum_scatter(
-            lax.dot_general(
-                weight_rows, cotangent, (((1,), (1,)), ((), ())), preferred_element_type=jnp.float32
-            ),
-            "tensor",
-            scatter_dimension=0,
-            tiled=True,
-        )
-    )
     adapter_backward = lax.dot_general(
         up_product_wide,
         adapter_a_flat,
@@ -110,13 +170,13 @@
     grad_b_part = grad_b_part.reshape(jobs_all, rank, local_width)
     count_part = jnp.sum(onehot, axis=0)
     grad_a, grad_b, token_counts = (
-        lax.psum_scatter(grad_a_part, "dp", scatter_dimension=0, tiled=True),
-        lax.psum_scatter(grad_b_part, "dp", scatter_dimension=0, tiled=True),
+        lax.psum_scatter(grad_a_part.astype(jnp.bfloat16), "dp", scatter_dimension=0, tiled=True),
+        lax.psum_scatter(grad_b_part.astype(jnp.bfloat16), "dp", scatter_dimension=0, tiled=True),
         lax.psum_scatter(count_part, "dp", scatter_dimension=0, tiled=True),
     )
     scale_factor = adapter_scale / token_counts
-    grad_a = grad_a * scale_factor[:, None, None]
-    grad_b = grad_b * scale_factor[:, None, None]
+    grad_a = grad_a.astype(jnp.float32) * scale_factor[:, None, None]
+    grad_b = grad_b.astype(jnp.float32) * scale_factor[:, None, None]
     new_a, new_a_first, new_a_second = adam_step(a_weight, a_first, a_second, grad_a)
     new_b, new_b_first, new_b_second = adam_step(b_weight, b_first, b_second, grad_b)
     return (

time: 685 us -> 360 us (0.53)
  waiting for transfers between devices: 513 us -> 106 us
  starting transfers between devices: 0.42 us -> 28.2 us
  matrix products: 85 us -> 108 us
  other arithmetic: 30.1 us -> 52.3 us
  local copies, waits for them, and re-layouts: 1.94 us -> 13.1 us
  blocking collectives: 39.4 us -> 30.8 us
    reduce_scatter x3 -> x2, waiting for transfers between devices: 387 us -> 0.01 us  [the longest x1 0.01 us: per_device(): lax.psum_scatter(grad_b_part.astype(jnp.bfloat16), 'dp', scatter_dimensio...]
    all_gather x1 -> x0, waiting for transfers between devices: 70.7 us -> none  [per_device(): lax.all_gather(tokens, 'tensor', axis=1, tiled=True)]
    ppermute x0 -> x8, waiting for transfers between devices: none -> 50.6 us  [the longest x4 32.6 us: grouped_sums(): from_left.append(lax.ppermute(right, 'tensor', to_right))]
    dot_general x2 -> x8, matrix products: 51.5 us -> 80.3 us  [the longest x3 37.3 us: grouped_sums(): jnp.dot(block, rows_of(owner), preferred_element_type=jnp.float32)]
    ppermute x0 -> x8, starting transfers between devices: none -> 28.1 us  [the longest x4 17.8 us: grouped_sums(): from_right.append(lax.ppermute(left, 'tensor', to_left))]
    convert_element_type x0 -> x4, other arithmetic: none -> 21.1 us  [the longest x3 17.1 us: outgoing(): return (came.astype(jnp.float32) + own).astype(jnp.bfloat16)]
    unnamed x15 -> x28, local copies, waits for them, and re-layouts: 1.24 us -> 12.4 us
    psum x1, blocking collectives: 33.1 us -> 24.6 us  [per_device(): down_proj = lax.psum(down_part, 'tensor')]
  transfers between devices with their start and end apart: 6 -> 12, of which waited for: 6 -> 10; matrix products, arithmetic and copies ran while one was open for 16% -> 43% of each run, Pallas kernels for 0% -> 0%
where the time goes in v1:
time: 360 us; the launch traced here: 353 us
  matrix products  108 us (30%)
  waiting for transfers between devices  106 us (29%)
  other arithmetic  52.3 us (15%)
  blocking collectives  30.8 us (9%)
  starting transfers between devices  28.2 us (8%)
  between operations  15.2 us (4%)
  local copies, waits for them, and re-layouts  13.1 us (4%)
    dot_general x3, matrix products, grouped_sums(): jnp.dot(block, rows_of(owner), preferred_element_type=jnp.float32)  37.3 us
    dot_general x4, matrix products, grouped_sums(): lax.dot_general(cotangent, out_weight[at * width:(at + 1) * width], (((1,...  33.2 us
    ppermute x4, waiting for transfers between devices, grouped_sums(): from_left.append(lax.ppermute(right, 'tensor', to_right))  32.6 us
    all_gather x1, waiting for transfers between devices, per_device(): lax.all_gather(adapter_b_half, 'dp', axis=0, tiled=True)  31.5 us
    psum x1, blocking collectives, per_device(): down_proj = lax.psum(down_part, 'tensor')  24.6 us
    all_gather x1, waiting for transfers between devices, per_device(): lax.all_gather(a_half, 'dp', axis=0, tiled=True)  23.5 us
    ppermute x4, waiting for transfers between devices, grouped_sums(): from_right.append(lax.ppermute(left, 'tensor', to_left))  18 us
    ppermute x4, starting transfers between devices, grouped_sums(): from_right.append(lax.ppermute(left, 'tensor', to_left))  17.8 us
  transfers between devices with their start and end apart: 12, of which 10 were waited for; matrix products, arithmetic and copies ran while one was open for 43% of the time, Pallas kernels for 0%

profile of v1, /device:TPU:0, one launch (start us, length us, event | category | flops | bytes accessed | tf_op | source)
XLA Modules:
  0.0 352.9 jit_solution(11780020189994411256)
XLA Ops:
  13.7 10.2 %select_select_fusion = s32[512]{0:T(512)S(1)} fusion(s32[512]{0:T(512)S(1)} %copy-done.7, s32[]{:T(128)} %bitcast.9, s32[]{:T(128)} %bitcast.10, s32[]{:T(128)} %bitcast.11, s32[]{:T(128)} %bitcast.12, s32[]{:T(128)} %bitcast.13, s32[]{:T(128)} %bitcast.14, s32[]{:T(128)} %bitcast.15, s32[]{:T(128)} %bitcast.16, s32[]{:T(128)} %bitcast.17, s32[]{:T(128)} %bitcast.18, ...), kind=kLoop, calls=%fused_computation.97 | loop fusion | flops 16896 | bytes 4160 | tf_op jit(solution)/shard_map/gather | solution.py:126
  23.9 23.5 %all-gather.3.cloned.1.call-done = bf16[16,2048,64]{1,2,0:T(8,128)(2,1)} async-done(((bf16[4,2048,64]{1,2,0:T(8,128)(2,1)}), bf16[16,2048,64]{1,2,0:T(8,128)(2,1)}) %all-gather.3.cloned.1.call-update) | async-done | bytes 4194320 | tf_op jit(solution)/shard_map/all_gather | solution.py:133
  47.4 5.2 %multiply_reduce_fusion.1 = f32[512,64]{0,1:T(8,128)S(1)} fusion(bf16[16,2048,64]{1,2,0:T(8,128)(2,1)} %all-gather.3.cloned.1.call-done, bf16[512,2048]{1,0:T(8,128)(2,1)} %param.11, f32[512,16]{0,1:T(8,128)S(1)} %fusion.89), kind=kOutput, calls=%fused_computation.63 | convolution fusion | flops 2148499456 | bytes 6455296 | tf_op jit(solution)/shard_map/dot_general | solution.py:139
  52.6 31.5 %all-gather.5.cloned.1.call-done = bf16[16,64,2048]{2,1,0:T(8,128)(2,1)} async-done(((bf16[4,64,2048]{2,1,0:T(8,128)(2,1)}), bf16[16,64,2048]{2,1,0:T(8,128)(2,1)}) %all-gather.5.cloned.1.call-update) | async-done | bytes 4194320 | tf_op jit(solution)/shard_map/all_gather | solution.py:134
  88.7 24.6 %all-reduce.3 = (bf16[512,64]{0,1:T(8,128)(2,1)S(1)}, bf16[512,64]{0,1:T(8,128)(2,1)S(1)}) all-reduce(f32[512,64]{0,1:T(8,128)S(1)} %multiply_reduce_fusion.1, f32[512,64]{0,1:T(8,128)S(1)} %multiply_reduce_fusion), channel_id=1, replica_groups=mesh['groups'=2,'dp'=4,'tensor'=4] {'tensor'}, use_global_device_ids=true, to_apply=%region_0.0 | all-reduce | flops 65536 | bytes 393216 | tf_op jit(solution)/shard_map/psum | solution.py:149
  125.8 8.3 %fusion.48 = bf16[1,512,2048]{1,2,0:T(8,128)(2,1)S(1)} fusion(bf16[512,2048]{1,0:T(8,128)(2,1)S(1)} %copy-done, bf16[8192,2048]{1,0:T(8,128)(2,1)} %param.15), kind=kOutput, calls=%fused_computation.53 | convolution fusion | flops 4296015872 | bytes 12582912 | tf_op jit(solution)/shard_map/dot_general | solution.py:38
  134.1 8.4 %fusion.51 = bf16[1,512,2048]{1,2,0:T(8,128)(2,1)S(1)} fusion(bf16[512,2048]{1,0:T(8,128)(2,1)S(1)} %copy-done, bf16[8192,2048]{1,0:T(8,128)(2,1)} %param.15), kind=kOutput, calls=%fused_computation.54 | convolution fusion | flops 4296015872 | bytes 12582912 | tf_op jit(solution)/shard_map/dot_general | solution.py:38
  142.5 8.3 %fusion.54 = bf16[1,512,2048]{1,2,0:T(8,128)(2,1)S(1)} fusion(bf16[512,2048]{1,0:T(8,128)(2,1)S(1)} %copy-done, bf16[8192,2048]{1,0:T(8,128)(2,1)} %param.15), kind=kOutput, calls=%fused_computation.55 | convolution fusion | flops 4296015872 | bytes 12582912 | tf_op jit(solution)/shard_map/dot_general | solution.py:38
  150.8 8.2 %fusion.45 = bf16[1,512,2048]{1,2,0:T(8,128)(2,1)S(1)} fusion(bf16[512,2048]{1,0:T(8,128)(2,1)S(1)} %copy-done, bf16[8192,2048]{1,0:T(8,128)(2,1)} %param.15), kind=kOutput, calls=%fused_computation.52 | convolution fusion | flops 4296015872 | bytes 12582912 | tf_op jit(solution)/shard_map/dot_general | solution.py:38
  164.6 5.4 %collective-permute-done = bf16[512,2048]{0,1:T(8,128)(2,1)} collective-permute-done((bf16[512,2048]{0,1:T(8,128)(2,1)}, bf16[512,2048]{0,1:T(8,128)(2,1)}, u32[]{:S(2)}, u32[]{:S(2)}) %collective-permute-start) | collective-permute-done | bytes 2097184 | tf_op jit(solution)/shard_map/ppermute | solution.py:64
  170.0 5.4 %fusion.29 = (bf16[512,2048]{0,1:T(8,128)(2,1)}, bf16[512,2048]{0,1:T(8,128)(2,1)}) fusion(bf16[512,2048]{0,1:T(8,128)(2,1)} %collective-permute-done.1, bf16[4,512,2048]{1,2,0:T(8,128)(2,1)S(1)} %pad_maximum_fusion, s32[]{:T(128)S(6)} %min.23, pred[]{:T(512)S(6)} %lt.51, s32[]{:T(128)S(6)} %min.22, pred[]{:T(512)S(6)} %lt.50, ...), kind=kLoop, calls=%fused_computation.38 | loop fusion | flops 10485760 | bytes 12582922 | tf_op jit(solution)/shard_map/convert_element_type | solution.py:55
  179.1 13.5 %collective-permute-start.2 = (bf16[512,2048]{0,1:T(8,128)(2,1)}, bf16[512,2048]{0,1:T(8,128)(2,1)}, u32[]{:S(2)}, u32[]{:S(2)}) collective-permute-start(bf16[512,2048]{0,1:T(8,128)(2,1)} %get-tuple-element.45), channel_id=1, source_target_pairs={{1,0},{2,1},{3,2},{5,4},{6,5},{7,6},{9,8},{10,9},{11,10},{13,12},{... | collective-permute-start | bytes 6291464 | tf_op jit(solution)/shard_map/ppermute | solution.py:64
  197.2 9.8 %fusion.14 = f32[2048,512]{1,0:T(8,128)} fusion(bf16[512,2048]{1,0:T(8,128)(2,1)S(1)} %copy-done.4, bf16[8192,2048]{1,0:T(8,128)(2,1)} %param.15, s32[]{:T(128)S(6)} %select_n.115), kind=kOutput, calls=%fused_computation.15 | convolution fusion | flops 4294967296 | bytes 14680068 | tf_op jit(solution)/shard_map/dot_general | solution.py:69
  207.0 10.9 %collective-permute-done.3 = bf16[512,2048]{0,1:T(8,128)(2,1)} collective-permute-done((bf16[512,2048]{0,1:T(8,128)(2,1)}, bf16[512,2048]{0,1:T(8,128)(2,1)}, u32[]{:S(2)}, u32[]{:S(2)}) %collective-permute-start.3) | collective-permute-done | bytes 2097184 | tf_op jit(solution)/shard_map/ppermute | solution.py:63
  217.9 5.4 %collective-permute-done.2 = bf16[512,2048]{0,1:T(8,128)(2,1)} collective-permute-done((bf16[512,2048]{0,1:T(8,128)(2,1)}, bf16[512,2048]{0,1:T(8,128)(2,1)}, u32[]{:S(2)}, u32[]{:S(2)}) %collective-permute-start.2) | collective-permute-done | bytes 2097184 | tf_op jit(solution)/shard_map/ppermute | solution.py:64
  223.3 6.8 %fusion.27 = (bf16[512,2048]{0,1:T(8,128)(2,1)}, bf16[512,2048]{0,1:T(8,128)(2,1)}) fusion(bf16[512,2048]{0,1:T(8,128)(2,1)} %collective-permute-done.3, bf16[4,512,2048]{1,2,0:T(8,128)(2,1)} %copy-done.2, s32[]{:T(128)S(6)} %min.26, pred[]{:T(512)S(6)} %lt.48, s32[]{:T(128)S(6)} %min.25, pred[]{:T(512)S(6)} %lt.53, bf16[512,2048]{0,1:T(8,128)(2,1)} %collective-permute-done.2), kind=kLoop, calls=%fused_computation.34 | loop fusion | flops 10485760 | bytes 12582922 | tf_op jit(solution)/shard_map/convert_element_type | solution.py:55
  234.3 6.1 %all-reduce = f32[16]{0:T(128)S(1)} all-reduce(f32[16]{0:T(128)S(1)} %fusion.90), channel_id=3, replica_groups=mesh['groups'=2,'dp'=4,'tensor'=4] {'dp'}, use_global_device_ids=true, to_apply=%region_4.5.clone | all-reduce | flops 16 | bytes 128
  240.5 10.7 %fusion.12 = f32[512,2048]{0,1:T(8,128)} fusion(bf16[8192,2048]{1,0:T(8,128)(2,1)} %param.15, s32[]{:T(128)S(6)} %select_n.119, bf16[512,2048]{0,1:T(8,128)(2,1)} %collective-permute-done, bf16[512,2048]{0,1:T(8,128)(2,1)} %collective-permute-done.1, pred[]{:T(512)S(6)} %lt.48), kind=kOutput, calls=%fused_computation.13 | convolution fusion | flops 4296015872 | bytes 16777220 | tf_op jit(solution)/shard_map/dot_general | solution.py:82
  251.2 10.7 %fusion.2 = f32[512,2048]{0,1:T(8,128)} fusion(bf16[8192,2048]{1,0:T(8,128)(2,1)} %param.15, s32[]{:T(128)S(6)} %select_n.127, bf16[512,2048]{0,1:T(8,128)(2,1)} %collective-permute-done.2, bf16[512,2048]{0,1:T(8,128)(2,1)} %collective-permute-done.3, pred[]{:T(512)S(6)} %lt.48), kind=kOutput, calls=%fused_computation.3 | convolution fusion | flops 4296015872 | bytes 16777220 | tf_op jit(solution)/shard_map/dot_general | solution.py:82
  261.9 9.0 %collective-permute-done.5 = bf16[512,2048]{0,1:T(8,128)(2,1)S(1)} collective-permute-done((bf16[512,2048]{0,1:T(8,128)(2,1)}, bf16[512,2048]{0,1:T(8,128)(2,1)S(1)}, u32[]{:S(2)}, u32[]{:S(2)}) %collective-permute-start.5) | collective-permute-done | bytes 2097184 | tf_op jit(solution)/shard_map/ppermute | solution.py:63
  288.4 15.9 %fusion.24 = bf16[512,2048]{0,1:T(8,128)(2,1)} fusion(f32[512,2048,1]{0,1,2:T(8,128)} %fusion.83, f32[512,2048]{0,1:T(8,128)} %fusion.2, f32[512,2048]{0,1:T(8,128)} %fusion.12, f32[2048,512]{1,0:T(8,128)} %fusion.14, bf16[8192,2048]{1,0:T(8,128)(2,1)} %param.15, s32[]{:T(128)S(6)} %select_n.139, bf16[512,2048]{0,1:T(8,128)(2,1)} %collective-permute-done.4, ...), kind=kOutput, calls=%fused_computation.30 | convolution fusion | flops 4304404480 | bytes 35651592 | tf_op jit(solution)/shard_map/dot_general | solution.py:82
  313.1 8.2 %collective-permute-done.6 = bf16[512,2048]{0,1:T(8,128)(2,1)S(1)} collective-permute-done((bf16[512,2048]{0,1:T(8,128)(2,1)}, bf16[512,2048]{0,1:T(8,128)(2,1)S(1)}, u32[]{:S(2)}, u32[]{:S(2)}) %collective-permute-start.6) | collective-permute-done | bytes 2097184 | tf_op jit(solution)/shard_map/ppermute | solution.py:63
  332.0 6.9 %divide_subtract_fusion = (f32[4,64,2048]{2,1,0:T(8,128)}, f32[4,64,2048]{2,1,0:T(8,128)}, f32[4,64,2048]{2,1,0:T(8,128)}) fusion(f32[4,64,2048]{2,1,0:T(8,128)} %param.17, f32[4]{0:T(128)S(1)} %dynamic-slice_divide_fusion, bf16[4,64,2048]{2,1,0:T(8,128)(2,1)} %reduce-scatter.5.cloned.1.call-done, f32[4,64,2048]{2,1,0:T(8,128)} %param.20, ...), kind=kLoop, calls=%fused_computation.64 | loop fusion | flops 7340032 | bytes 13631504 | tf_op jit(solution)/shard_map/sub | solution.py:18
  338.9 7.0 %divide_subtract_fusion.1 = (f32[4,2048,64]{1,2,0:T(8,128)}, f32[4,2048,64]{1,2,0:T(8,128)}, f32[4,2048,64]{1,2,0:T(8,128)}) fusion(f32[4,2048,64]{1,2,0:T(8,128)} %param.16, f32[4]{0:T(128)S(1)} %dynamic-slice_divide_fusion, bf16[4,2048,64]{1,2,0:T(8,128)(2,1)} %reduce-scatter.3.cloned.1.call-done, f32[4,2048,64]{1,2,0:T(8,128)} %param.18, ...), kind=kLoop, calls=%fused_computation.67 | loop fusion | flops 7340032 | bytes 13631504 | tf_op jit(solution)/shard_map/sub | solution.py:18
  (66 shorter events, 77.7 us)
Async XLA Ops:
  7.2 77.0 %copy-start = (bf16[512,2048]{1,0:T(8,128)(2,1)S(1)}, bf16[512,2048]{1,0:T(8,128)(2,1)}, u32[]{:S(2)}) copy-start(bf16[512,2048]{1,0:T(8,128)(2,1)} %param.12) | copy-start | bytes 6291460
  7.2 40.3 %all-gather.3.cloned.1.call-start = ((), (), s32[]{:S(2)}) async-start(), calls=%async_computation.2 | async-start | bytes 5242880 | tf_op jit(solution)/shard_map/all_gather | solution.py:133
  10.1 2.9 copy-start.6
  10.1 3.6 %copy-start.7 = (s32[512]{0:T(512)S(1)}, s32[512]{0:T(512)}, u32[]{:S(2)}) copy-start(s32[512]{0:T(512)} %param.13) | copy-start | bytes 6148
  10.1 74.0 %all-gather.5.cloned.1.call-start = ((), (), s32[]{:S(2)}) async-start(), calls=%async_computation.3 | async-start | bytes 5242880 | tf_op jit(solution)/shard_map/all_gather | solution.py:134
  12.9 319.1 %reduce-scatter.5.cloned.1.call-start = ((), (), s32[]{:S(2)}) async-start(), calls=%async_computation.5 | async-start | bytes 5242880 | tf_op jit(solution)/shard_map/reduce_scatter | solution.py:174
  117.6 221.2 %reduce-scatter.3.cloned.1.call-start = ((), (), s32[]{:S(2)}) async-start(), calls=%async_computation.4 | async-start | bytes 5242880 | tf_op jit(solution)/shard_map/reduce_scatter | solution.py:173
  121.6 43.0 %collective-permute-start.1 = (bf16[512,2048]{0,1:T(8,128)(2,1)}, bf16[512,2048]{0,1:T(8,128)(2,1)}, u32[]{:S(2)}, u32[]{:S(2)}) collective-permute-start(bf16[512,2048]{0,1:T(8,128)(2,1)} %copy.45), channel_id=1, source_target_pairs={{0,1},{1,2},{2,3},{4,5},{5,6},{6,7},{8,9},{9,10},{10,11},{12,13},{... | collective-permute-start | bytes 6291464 | tf_op jit(solution)/shard_map/ppermute | solution.py:63
  124.2 45.8 %collective-permute-start = (bf16[512,2048]{0,1:T(8,128)(2,1)}, bf16[512,2048]{0,1:T(8,128)(2,1)}, u32[]{:S(2)}, u32[]{:S(2)}) collective-permute-start(bf16[512,2048]{0,1:T(8,128)(2,1)} %copy.45), channel_id=1, source_target_pairs={{1,0},{2,1},{3,2},{5,4},{6,5},{7,6},{9,8},{10,9},{11,10},{13,12},{... | collective-permute-start | bytes 6291464 | tf_op jit(solution)/shard_map/ppermute | solution.py:64
  160.1 15.3 %copy-start.2 = (bf16[4,512,2048]{1,2,0:T(8,128)(2,1)}, bf16[4,512,2048]{1,2,0:T(8,128)(2,1)S(1)}, u32[]{:S(2)}) copy-start(bf16[4,512,2048]{1,2,0:T(8,128)(2,1)S(1)} %pad_maximum_fusion) | copy-start | bytes 25165828
  160.1 32.7 %copy-start.4 = (bf16[512,2048]{1,0:T(8,128)(2,1)S(1)}, bf16[512,2048]{1,0:T(8,128)(2,1)}, u32[]{:S(2)}) copy-start(bf16[512,2048]{1,0:T(8,128)(2,1)} %param.11) | copy-start | bytes 6291460
  175.4 42.4 %collective-permute-start.3 = (bf16[512,2048]{0,1:T(8,128)(2,1)}, bf16[512,2048]{0,1:T(8,128)(2,1)}, u32[]{:S(2)}, u32[]{:S(2)}) collective-permute-start(bf16[512,2048]{0,1:T(8,128)(2,1)} %get-tuple-element.44), channel_id=1, source_target_pairs={{0,1},{1,2},{2,3},{4,5},{5,6},{6,7},{8,9},{9,10},{10,11},{12,13},{... | collective-permute-start | bytes 6291464 | tf_op jit(solution)/shard_map/ppermute | solution.py:63
  179.1 44.2 %collective-permute-start.2 = (bf16[512,2048]{0,1:T(8,128)(2,1)}, bf16[512,2048]{0,1:T(8,128)(2,1)}, u32[]{:S(2)}, u32[]{:S(2)}) collective-permute-start(bf16[512,2048]{0,1:T(8,128)(2,1)} %get-tuple-element.45), channel_id=1, source_target_pairs={{1,0},{2,1},{3,2},{5,4},{6,5},{7,6},{9,8},{10,9},{11,10},{13,12},{... | collective-permute-start | bytes 6291464 | tf_op jit(solution)/shard_map/ppermute | solution.py:64
  207.0 26.1 %copy-start.9 = (u32[32]{0:T(128)S(1)}, u32[32]{0:T(128)}, u32[]{:S(2)}) copy-start(u32[32]{0:T(128)} %constant.108) | copy-start | bytes 388
  230.1 40.9 %collective-permute-start.5 = (bf16[512,2048]{0,1:T(8,128)(2,1)}, bf16[512,2048]{0,1:T(8,128)(2,1)S(1)}, u32[]{:S(2)}, u32[]{:S(2)}) collective-permute-start(bf16[512,2048]{0,1:T(8,128)(2,1)} %get-tuple-element.42), channel_id=1, source_target_pairs={{0,1},{1,2},{2,3},{4,5},{5,6},{6,7},{8,9},{9,10},{10,11},{12,13},{... | collective-permute-start | bytes 6291464 | tf_op jit(solution)/shard_map/ppermute | solution.py:63
  231.6 43.6 %collective-permute-start.4 = (bf16[512,2048]{0,1:T(8,128)(2,1)}, bf16[512,2048]{0,1:T(8,128)(2,1)}, u32[]{:S(2)}, u32[]{:S(2)}) collective-permute-start(bf16[512,2048]{0,1:T(8,128)(2,1)} %get-tuple-element.43), channel_id=1, source_target_pairs={{1,0},{2,1},{3,2},{5,4},{6,5},{7,6},{9,8},{10,9},{11,10},{13,12},{... | collective-permute-start | bytes 6291464 | tf_op jit(solution)/shard_map/ppermute | solution.py:64
  240.5 34.7 %slice-start = ((s8[8388608]{0:T(1024)(128)(4,1)}), s8[4194304]{0:T(1024)(128)(4,1)S(1)}, s32[]{:S(2)}) async-start(s8[8388608]{0:T(1024)(128)(4,1)} %bitcast.117), calls=%async_computation.6 | async-start | bytes 8388608
  251.2 24.0 %slice-start.1 = ((s8[8388608]{0:T(1024)(128)(4,1)}), s8[4194304]{0:T(1024)(128)(4,1)S(1)}, s32[]{:S(2)}) async-start(s8[8388608]{0:T(1024)(128)(4,1)} %bitcast.117), calls=%async_computation.7 | async-start | bytes 8388608
  261.9 22.1 %copy-start.8 = (bf16[16,64,2048]{2,1,0:T(8,128)(2,1)S(1)}, bf16[16,64,2048]{2,1,0:T(8,128)(2,1)}, u32[]{:S(2)}) copy-start(bf16[16,64,2048]{2,1,0:T(8,128)(2,1)} %all-gather.5.cloned.1.call-done) | copy-start | bytes 12582916
  271.0 9.1 %copy-start.5 = (bf16[512,2048]{0,1:T(8,128)(2,1)}, bf16[512,2048]{0,1:T(8,128)(2,1)S(1)}, u32[]{:S(2)}) copy-start(bf16[512,2048]{0,1:T(8,128)(2,1)S(1)} %collective-permute-done.5) | copy-start | bytes 6291460
  280.0 41.3 %collective-permute-start.6 = (bf16[512,2048]{0,1:T(8,128)(2,1)}, bf16[512,2048]{0,1:T(8,128)(2,1)S(1)}, u32[]{:S(2)}, u32[]{:S(2)}) collective-permute-start(bf16[512,2048]{0,1:T(8,128)(2,1)} %get-tuple-element.40), channel_id=1, source_target_pairs={{0,1},{1,2},{2,3},{4,5},{5,6},{6,7},{8,9},{9,10},{10,11},{12,13},{... | collective-permute-start | bytes 6291464 | tf_op jit(solution)/shard_map/ppermute | solution.py:63
  282.6 43.0 %collective-permute-start.7 = (bf16[512,2048]{0,1:T(8,128)(2,1)}, bf16[512,2048]{0,1:T(8,128)(2,1)}, u32[]{:S(2)}, u32[]{:S(2)}) collective-permute-start(bf16[512,2048]{0,1:T(8,128)(2,1)} %get-tuple-element.41), channel_id=1, source_target_pairs={{1,0},{2,1},{3,2},{5,4},{6,5},{7,6},{9,8},{10,9},{11,10},{13,12},{... | collective-permute-start | bytes 6291464 | tf_op jit(solution)/shard_map/ppermute | solution.py:64
  321.3 1.3 copy-start.3
  338.9 7.0 %copy-start.1 = (bf16[512,2048]{1,0:T(8,128)(2,1)S(1)}, bf16[512,2048]{1,0:T(8,128)(2,1)}, u32[]{:S(2)}) copy-start(bf16[512,2048]{1,0:T(8,128)(2,1)} %param.12) | copy-start | bytes 6291460
Sparse Core Ops, SparseCore 0:
  10.2 37.1 all-gather.2
  49.6 34.5 all-gather.4
  117.8 42.0 reduce-scatter.4
  197.3 43.8 reduce-scatter.2
